TPU v7x, 128 devices: a whole 4x4x4 slice. The times are simulated.
128 devices in a mesh: rep: 16 (over x_lo, y, core), exp: 8 (over x_hi, z).
Axes of the slice: x: 4 (x_hi: 2, x_lo: 2; x = x_hi * 2 + x_lo), y: 4, z: 4, core: 2. Of those that a mesh axis runs over, the one named last changes fastest.
Arguments:
- grad_out: bfloat16 [16384, 3072], P(('rep', 'exp')), may hold values from -6 to 6
- routes: int32 [16384, 2], P(('rep', 'exp')), may hold values from 0 to 7, all different within a row; in each aligned block of 128 rows (0 to 127, 128 to 255, ...) at most 36 rows name the same one
- probs: float32 [16384, 2], P(('rep', 'exp')), may hold values from 0.2 to 1
- rows_hidden: bfloat16 [8, 4608, 8192], P('exp', None, 'rep'), may hold values from -6 to 6
- w_down: bfloat16 [8, 8192, 3072], P('exp', 'rep'), may hold values from -0.0625 to 0.0625
Outputs:
- d_rows: bfloat16 [8, 4608, 8192], P('exp', None, 'rep')
- grad_down: bfloat16 [8, 8192, 3072], P('exp', 'rep')
Inputs may be any that keep to these rules, and one draw needn't show every extreme that they name: The two experts of a token differ; within each device's block of 128 tokens no expert is named by more than 36 routes, a bound that some block reaches.
All inputs are finite; a program needn't handle non-finite values.
Results may differ from a plain program's by a relative error of at most 0.005.
Values may be sent and summed in bfloat16 or wider, within the bound.
A program may use at most 192 MiB of HBM per device.

v0:
```python
import jax
import jax.numpy as jnp
from jax import lax
from jax.sharding import PartitionSpec as P

CAP = 36


def per_device(grad_out, routes, probs, rows_hidden, w_down):
    owned = w_down.shape[0]
    hid_width = w_down.shape[1]
    model_width = grad_out.shape[1]
    tok_count = grad_out.shape[0]
    rep_count = lax.axis_size("rep")
    exp_count = lax.axis_size("exp")
    experts = owned * exp_count
    block_count = rep_count * exp_count
    route_list = routes.reshape(tok_count * 2)
    onehot = (route_list[:, None] == jnp.arange(experts, dtype=jnp.int32)[None, :]).astype(
        jnp.int32
    )
    before = jnp.cumsum(onehot, axis=0) - onehot
    slot_index = jnp.sum(before * onehot, axis=1)
    target = route_list * CAP + slot_index
    scaled = (
        probs.reshape(tok_count * 2, 1) * jnp.repeat(grad_out, 2, axis=0).astype(jnp.float32)
    ).astype(jnp.bfloat16)
    send_cot = jnp.zeros((experts * CAP, model_width), jnp.bfloat16).at[target].set(scaled)
    hidden_blocks = rows_hidden.reshape(owned, block_count, CAP, hid_width)
    send_cot = send_cot.reshape(exp_count, owned, CAP, model_width)
    own_cot = lax.all_to_all(send_cot, "exp", split_axis=0, concat_axis=0, tiled=True)
    piece = lax.all_gather(own_cot, "rep", axis=0, tiled=True)
    d_part = jnp.einsum("nlcd,lhd->lnch", piece, w_down, preferred_element_type=jnp.float32).astype(
        jnp.bfloat16
    )
    d_all = d_part
    grad_sum = jnp.einsum(
        "lnch,nlcd->lhd", hidden_blocks, piece, preferred_element_type=jnp.float32
    )
    d_all, grad_sum = (d_all, grad_sum)
    d_rows = d_all.reshape(owned, block_count * CAP, hid_width)
    return (d_rows, grad_sum.astype(jnp.bfloat16))


def solution(mesh):
    return jax.shard_map(
        per_device,
        mesh=mesh,
        in_specs=(
            P(("rep", "exp"), None),
            P(("rep", "exp"), None),
            P(("rep", "exp"), None),
            P("exp", None, "rep"),
            P("exp", "rep", None),
        ),
        out_specs=(P("exp", None, "rep"), P("exp", "rep", None)),
        check_vma=False,
    )
```

profile of v0, /device:TPU:1, one launch (start us, length us, event | category | flops | bytes accessed | tf_op | source)
XLA Modules:
  0.0 275.4 jit_solution(16191494713234691535)
XLA Ops:
  7.2 0.0 copy-start
  7.2 0.0 all-gather.2.cloned.1.call-start
  7.2 0.8 broadcast_multiply_fusion
  8.1 0.9 copy.20
  8.9 0.1 eq.29
  9.1 0.1 eq.25
  9.2 0.1 copy.19
  9.3 0.1 mul.31
  9.5 0.6 reduce-window.6
  10.1 0.2 slice_reduce_fusion
  10.3 0.8 copy.22
  11.1 0.1 mul.33
  11.2 3.6 %broadcast_in_dim.9 = f32[128,2,3072]{2,1,0:T(2,128)} broadcast(bf16[128,3072]{1,0:T(8,128)(2,1)} %param.5), dimensions={0,2} | broadcast | bytes 3932160 | tf_op jit(solution)/shard_map/broadcast_in_dim | solution.py:26
  14.9 5.2 %convert_element_type.33 = f32[256,3072]{1,0:T(8,128)} reshape(f32[128,2,3072]{2,1,0:T(2,128)} %broadcast_in_dim.9) | data formatting | bytes 6291456 | tf_op jit(solution)/shard_map/convert_element_type | solution.py:26
  20.1 0.1 fusion.22
  20.2 5.5 %scatter_custom_fusion = bf16[288,3072]{1,0:T(8,128)(2,1)} fusion(s32[256]{0:T(256)S(1)} %bitcast.39, f32[256,3072]{1,0:T(8,128)} %convert_element_type.33, f32[256]{0:T(256)S(1)} %mul.33, bf16[]{:T(256)} %constant.4.clone.1), kind=kCustom, calls=%fused_computation.11 | custom fusion | flops 1572864 | bytes 4916226 | tf_op jit(solution)/shard_map/scatter | solution.py:28
  25.7 2.6 reshape.78
  28.3 33.8 %all_to_all.5 = bf16[8,1,36,3072]{3,2,1,0:T(8,128)(2,1)S(1)} all-to-all(bf16[8,1,36,3072]{3,2,1,0:T(8,128)(2,1)} %bitcast.37), channel_id=1, replica_groups=mesh['rep'=16,'exp'=8] {'exp'}, dimensions={0} | all-to-all | bytes 3538944 | tf_op jit(solution)/shard_map/all_to_all | solution.py:31
  62.1 2.2 copy.24
  64.3 0.0 all-gather.2.cloned.1.call-update
  64.3 7.9 %reshape.82 = bf16[128,36,512]{2,1,0:T(8,128)(2,1)} reshape(bf16[1,4608,512]{2,1,0:T(8,128)(2,1)} %param.8) | data formatting | bytes 9437184 | tf_op jit(solution)/shard_map/reshape.12
  72.2 137.8 %all-gather.2.cloned.1.call-done = bf16[128,1,36,3072]{3,0,2,1:T(8,128)(2,1)} async-done(((bf16[8,1,36,3072]{3,0,2,1:T(8,128)(2,1)}), bf16[128,1,36,3072]{3,0,2,1:T(8,128)(2,1)}) %all-gather.2.cloned.1.call-update) | async-done | bytes 28311568 | tf_op jit(solution)/shard_map/all_gather | solution.py:32
  210.0 0.0 copy-done
  210.0 19.0 %fusion.13 = bf16[128,36,512]{2,0,1:T(8,128)(2,1)S(1)} fusion(bf16[1,512,3072]{2,1,0:T(8,128)(2,1)S(1)} %copy-done, bf16[128,1,36,3072]{3,0,2,1:T(8,128)(2,1)} %all-gather.2.cloned.1.call-done), kind=kOutput, calls=%fused_computation.10 | convolution fusion | flops 14497873920 | bytes 36175872 | tf_op jit(solution)/shard_map/nlcd,lhd->lnch/dot_general | solution.py:33
  229.0 5.2 %copy.25 = bf16[128,36,512]{2,1,0:T(8,128)(2,1)} copy(bf16[128,36,512]{2,0,1:T(8,128)(2,1)S(1)} %fusion.13) | data formatting | bytes 9437184 | tf_op jit(solution)/shard_map/convert_element_type | solution.py:33
  234.2 7.9 %reshape.81 = bf16[1,4608,512]{2,1,0:T(8,128)(2,1)} reshape(bf16[128,36,512]{2,1,0:T(8,128)(2,1)} %copy.25) | data formatting | bytes 9437184 | tf_op jit(solution)/shard_map/reshape | solution.py:41
  242.1 0.0 copy-start.1
  242.1 21.8 %fusion.7 = bf16[1,512,3072]{1,2,0:T(8,128)(2,1)} fusion(bf16[128,36,512]{2,1,0:T(8,128)(2,1)} %reshape.82, bf16[128,1,36,3072]{3,0,2,1:T(8,128)(2,1)} %all-gather.2.cloned.1.call-done), kind=kOutput, calls=%fused_computation.7 | convolution fusion | flops 14497087488 | bytes 36175872 | tf_op jit(solution)/shard_map/lnch,nlcd->lhd/dot_general | solution.py:37
  263.9 4.6 %copy.28 = bf16[1,512,3072]{2,1,0:T(8,128)(2,1)} copy(bf16[1,512,3072]{1,2,0:T(8,128)(2,1)} %fusion.7) | data formatting | bytes 6291456
  268.6 0.0 copy-done.1
  (4 shorter events, 0.1 us)
Async XLA Ops:
  7.2 202.8 %copy-start = (bf16[1,512,3072]{2,1,0:T(8,128)(2,1)S(1)}, bf16[1,512,3072]{2,1,0:T(8,128)(2,1)}, u32[]{:S(2)}) copy-start(bf16[1,512,3072]{2,1,0:T(8,128)(2,1)} %param.9) | copy-start | bytes 9437188
  7.2 202.8 %all-gather.2.cloned.1.call-start = ((), (), s32[]{:S(2)}) async-start(), calls=%async_computation.1 | async-start | bytes 30081024 | tf_op jit(solution)/shard_map/all_gather | solution.py:32
  242.1 26.5 %copy-start.1 = (bf16[1,512,3072]{2,1,0:T(8,128)(2,1)S(1)}, bf16[1,512,3072]{2,1,0:T(8,128)(2,1)}, u32[]{:S(2)}) copy-start(bf16[1,512,3072]{2,1,0:T(8,128)(2,1)} %param.9) | copy-start | bytes 9437188
Sparse Core Ops, SparseCore 0:
  64.5 145.4 all-gather.1
where the time goes:
time: 276 us; the launch traced here: 275 us
  waiting for transfers between devices  138 us (50%)
  local copies, waits for them, and re-layouts  41.8 us (15%)
  matrix products  40.9 us (15%)
  blocking collectives  33.8 us (12%)
  between operations  14.1 us (5%)
  other arithmetic  7.1 us (3%)
    all_gather x1, waiting for transfers between devices, per_device(): piece = lax.all_gather(own_cot, 'rep', axis=0, tiled=True)  138 us
    all_to_all x1, blocking collectives, per_device(): lax.all_to_all(send_cot, 'exp', split_axis=0, concat_axis=0, tiled=True)  33.8 us
    dot_general x1, matrix products, per_device(): jnp.einsum('lnch,nlcd->lhd', hidden_blocks, piece, preferred_element_type...  21.8 us
    dot_general x1, matrix products, per_device(): jnp.einsum('nlcd,lhd->lnch', piece, w_down, preferred_element_type=jnp.fl...  19 us
    reshape x1, local copies, waits for them, and re-layouts, per_device(): d_rows = d_all.reshape(owned, block_count * CAP, hid_width)  7.9 us
    another operation x2, local copies, waits for them, and re-layouts  7.89 us
    unnamed x7, local copies, waits for them, and re-layouts  6.3 us
    scatter x1, other arithmetic, per_device(): jnp.zeros((experts * CAP, model_width), jnp.bfloat16).at[target].set(scaled)  5.54 us
  transfers between devices with their start and end apart: 1, of which 1 were waited for; matrix products, arithmetic and copies ran while one was open for 3% of the time, Pallas kernels for 0%

commit v1 on v0

v1 whole, which is shorter than its diff:
```python
import jax
import jax.numpy as jnp
from jax import lax
from jax.experimental import pallas as pl
from jax.experimental.pallas import tpu as pltpu
from jax.sharding import PartitionSpec as P

CAP = 36
EXPERTS = 8
TOK = 128
D = 3072
FFD = 512
ROWS = 4608
W = 256
C = D // W
WIN = 48
GRP = 4 * CAP
UNIT = 2 * GRP
NU = 16
A = 160
A1 = 64
BR = UNIT - A
MESH = pl.DeviceIdType.MESH

LEXP, L1, L2, L3, LCORE = range(5)


def gather_kernel(
    rt_ref, pt_ref, g_hbm, h_hbm, w_hbm, d_hbm, gd_hbm,
    dy, send, recv, hb, ht, wv, gv, acc, gst, sel, prow,
    ssem, rsem, lsem, osem,
):
    rep = lax.axis_index("rep")
    ex = lax.axis_index("exp")
    lo, y, core = rep // 8, (rep // 2) % 4, rep % 2
    hi, z = ex // 4, ex % 4

    def unit(dl, dyy):
        return ((lo + dl) % 2 * 4 + (y + dyy + 4) % 4) * 2 + core

    to_x = (unit(1, 0), ex)
    to_yp = (unit(0, 1), ex)
    to_ym = (unit(0, -1), ex)
    to_core = ((lo * 4 + y) * 2 + 1 - core, ex)
    spread = []
    for dh in range(2):
        for dz in range(4):
            if dh or dz:
                hz = (hi + dh) % 2 * 4 + (z + dz) % 4
                spread.append((dh, (unit(dh, 0), hz), hz))
    peers = [to_x, to_yp, to_ym, to_core] + [s[1] for s in spread]

    load_g = pltpu.make_async_copy(g_hbm, gv, lsem.at[0])
    load_w = pltpu.make_async_copy(w_hbm.at[0], wv, lsem.at[1])
    load_g.start()

    bar = pltpu.get_barrier_semaphore()
    for p in peers:
        pl.semaphore_signal(bar, inc=1, device_id=p, device_id_type=MESH)

    def group_rows(i):
        u, part = i // 2, i % 2
        r = (u + 8 * part) % 16
        g = r * 2 + (hi + part) % 2
        return pl.multiple_of(g * GRP, 16)

    def start_hidden(i, _):
        pltpu.make_async_copy(
            h_hbm.at[0, pl.ds(group_rows(i), GRP)],
            hb.at[pl.ds(pl.multiple_of(i * GRP, 16), GRP)],
            lsem.at[2],
        ).start()
        return 0

    rt = rt_ref[...]
    pt = pt_ref[...]
    erow = lax.broadcasted_iota(jnp.int32, (EXPERTS, TOK), 0)
    oh0 = (rt[0:1] == erow).astype(jnp.float32)
    oh1 = (rt[1:2] == erow).astype(jnp.float32)
    upper = (
        lax.broadcasted_iota(jnp.int32, (TOK, TOK), 0)
        < lax.broadcasted_iota(jnp.int32, (TOK, TOK), 1)
    ).astype(jnp.float32)
    before = jnp.dot(oh0 + oh1, upper, preferred_element_type=jnp.float32)
    slot0 = jnp.sum(oh0 * before, axis=0, keepdims=True).astype(jnp.int32)
    slot1 = jnp.sum(oh1 * before, axis=0, keepdims=True).astype(jnp.int32)
    t0 = rt[0:1] * WIN + slot0 + 4 * z
    t1 = rt[1:2] * WIN + slot1 + 4 * z
    row = lax.broadcasted_iota(jnp.int32, (EXPERTS * WIN, TOK), 0)
    m0 = row == t0
    m1 = row == t1
    sel[...] = (m0 | m1).astype(jnp.float32).astype(jnp.bfloat16)
    pw = jnp.where(m0, pt[0:1], 0.0) + jnp.where(m1, pt[1:2], 0.0)
    prow[...] = jnp.broadcast_to(jnp.sum(pw, axis=1, keepdims=True), prow.shape)

    def remote(src, dst, stage, c, device):
        return pltpu.make_async_remote_copy(
            src_ref=src, dst_ref=dst, send_sem=ssem.at[stage, c], recv_sem=rsem.at[stage, c],
            device_id=device, device_id_type=MESH,
        )

    def wait_rows(sem, c, rows):
        ref = dy.at[c, pl.ds(0, rows)]
        pltpu.make_async_copy(ref, ref, sem).wait()

    def push(stage, c, u, start, rows, device):
        ref = dy.at[c, pl.ds(pl.multiple_of(u * UNIT + start, 16), rows)]
        remote(ref, ref, stage, c, device).start()

    def prep(c):
        g = gv[:, pl.ds(pl.multiple_of(c * W, W), W)]
        rows = jnp.dot(sel[...], g, preferred_element_type=jnp.float32)
        for i in range(W // 128):
            cols = slice(i * 128, (i + 1) * 128)
            send[c, :, cols] = (rows[:, cols] * prow[...]).astype(jnp.bfloat16)
        for dh, device, e in spread:
            remote(
                send.at[c, pl.ds(pl.multiple_of(e * WIN, 16), WIN)],
                recv.at[c, dh * 4 + z],
                LEXP, c, device,
            ).start()
        recv[c, z] = send[c, pl.ds(pl.multiple_of(ex * WIN, 16), WIN), :]

    def stage1(c):
        ref = recv.at[c, pl.ds(0, 7)]
        pltpu.make_async_copy(ref, ref, rsem.at[LEXP, c]).wait()
        base = rep * UNIT
        for part in range(2):
            for s in range(4):
                at = pl.multiple_of(base + part * GRP + s * 32, 16)
                if s == 0:
                    dy[c, pl.ds(at, 16), :] = recv[c, part * 4, 0:16, :]
                else:
                    dy[c, pl.ds(at, 16), :] = (
                        recv[c, part * 4 + s - 1, 32:48, :] + recv[c, part * 4 + s, 0:16, :]
                    )
                dy[c, pl.ds(pl.multiple_of(at + 16, 16), 16), :] = recv[c, part * 4 + s, 16:32, :]
                if s == 3:
                    dy[c, pl.ds(pl.multiple_of(at + 32, 16), 16), :] = recv[c, part * 4 + s, 32:48, :]
        for device in (to_x, to_yp, to_ym):
            push(L1, c, rep, 0, UNIT, device)
        push(LCORE, c, rep, 0, UNIT, to_core)

    def stage2(c):
        wait_rows(rsem.at[L1, c], c, 3 * UNIT)
        push(L2, c, unit(0, -1), 0, A, to_yp)
        push(L2, c, unit(0, 1), A, BR, to_ym)
        push(L2, c, unit(0, 1), A, BR, to_x)
        push(L2, c, unit(1, 0), 0, A, to_yp)
        push(L2, c, unit(1, 0), 0, A, to_ym)
        push(L2, c, unit(0, -1), A, BR, to_x)
        for u in (unit(1, 0), unit(0, 1), unit(0, -1)):
            push(LCORE, c, u, 0, UNIT, to_core)

    def stage3(c):
        wait_rows(rsem.at[L2, c], c, 3 * UNIT)
        push(L3, c, unit(1, -1), 0, A1, to_yp)
        push(L3, c, unit(1, 1), A1, A - A1, to_ym)
        push(L3, c, unit(0, 2), A, BR, to_x)
        for u in (unit(0, 2), unit(1, 1), unit(1, -1)):
            push(LCORE, c, u, 0, UNIT, to_core)

    def stage4(c):
        wait_rows(rsem.at[L3, c], c, UNIT)
        push(LCORE, c, unit(1, 2), 0, UNIT, to_core)

    def out_grad(c):
        return pltpu.make_async_copy(
            gst.at[c % 2],
            gd_hbm.at[0, :, pl.ds(pl.multiple_of(c * W, W), W)],
            osem.at[c % 2],
        )

    blk = 1152

    def d_block(c, i):
        at = pl.ds(pl.multiple_of(i * blk, blk), blk)
        wc = wv[:, pl.ds(pl.multiple_of(c * W, W), W)]
        return at, lax.dot_general(
            dy[c, at, :], wc, (((1,), (1,)), ((), ())), preferred_element_type=jnp.float32
        )

    def compute(c):
        wait_rows(rsem.at[LCORE, c], c, 8 * UNIT)

        @pl.when(c >= 2)
        def _():
            out_grad(c - 2).wait()

        gst[c % 2] = jnp.dot(ht[...], dy[c], preferred_element_type=jnp.float32).astype(jnp.bfloat16)
        out_grad(c).start()

        @pl.when(c < C - 1)
        def _():
            def body(i, _):
                at, part = d_block(c, i)
                acc[at, :] += part
                return 0

            lax.fori_loop(0, ROWS // blk, body, 0)

        @pl.when(c == C - 1)
        def _():
            def body(i, _):
                at, part = d_block(c, i)
                hb[at, :] = (acc[at, :] + part).astype(jnp.bfloat16)

                def put(k, _):
                    n = i * (blk // GRP) + k
                    pltpu.make_async_copy(
                        hb.at[pl.ds(pl.multiple_of(n * GRP, 16), GRP)],
                        d_hbm.at[0, pl.ds(group_rows(n), GRP)],
                        lsem.at[3],
                    ).start()
                    return 0

                lax.fori_loop(0, blk // GRP, put, 0)
                return 0

            lax.fori_loop(0, ROWS // blk, body, 0)

    load_g.wait()
    pl.semaphore_wait(bar, len(peers))
    prep(0)
    prep(1)
    lax.fori_loop(0, 32, start_hidden, 0)
    load_w.start()

    def turn_hidden():
        pltpu.make_async_copy(hb, hb, lsem.at[2]).wait()

        def body(i, _):
            at = pl.ds(pl.multiple_of(i * 128, 128), 128)
            ht[:, at] = hb[at, :].T
            return 0

        lax.fori_loop(0, ROWS // 128, body, 0)
        acc[...] = jnp.zeros_like(acc)
        load_w.wait()

    def step(t, _):
        def stage(lag, fn, ahead=0):
            c = t - lag + ahead

            @pl.when((c >= 0) & (c < C))
            def _():
                fn(c)

        stage(0, stage1)
        stage(1, stage2)
        stage(2, stage3)
        stage(3, stage4)

        @pl.when(t + 2 < C)
        def _():
            prep(t + 2)

        pl.when(t == 1)(turn_hidden)
        stage(4, compute)
        return 0

    lax.fori_loop(0, C + 4, step, 0)

    def drain(c, _):
        ref = recv.at[c, pl.ds(0, 7)]
        pltpu.make_async_copy(ref, ref, ssem.at[LEXP, c]).wait()
        wait_rows(ssem.at[L1, c], c, 3 * UNIT)
        wait_rows(ssem.at[L2, c], c, 3 * UNIT)
        wait_rows(ssem.at[L3, c], c, UNIT)
        wait_rows(ssem.at[LCORE, c], c, 8 * UNIT)
        return 0

    lax.fori_loop(0, C, drain, 0)
    out_grad(C - 2).wait()
    out_grad(C - 1).wait()
    pltpu.make_async_copy(hb, hb, lsem.at[3]).wait()


def per_device(grad_out, routes, probs, rows_hidden, w_down):
    bf = jnp.bfloat16
    any_spec = pl.BlockSpec(memory_space=pl.ANY)
    vmem = pl.BlockSpec(memory_space=pltpu.VMEM)
    return pl.pallas_call(
        gather_kernel,
        out_shape=(
            jax.ShapeDtypeStruct((1, ROWS, FFD), bf),
            jax.ShapeDtypeStruct((1, FFD, D), bf),
        ),
        in_specs=[vmem, vmem, any_spec, any_spec, any_spec],
        out_specs=(any_spec, any_spec),
        scratch_shapes=[
            pltpu.VMEM((C, ROWS, W), bf),
            pltpu.VMEM((C, EXPERTS * WIN, W), bf),
            pltpu.VMEM((C, 8, WIN, W), bf),
            pltpu.VMEM((ROWS, FFD), bf),
            pltpu.VMEM((FFD, ROWS), bf),
            pltpu.VMEM((FFD, D), bf),
            pltpu.VMEM((TOK, D), bf),
            pltpu.VMEM((ROWS, FFD), jnp.float32),
            pltpu.VMEM((2, FFD, W), bf),
            pltpu.VMEM((EXPERTS * WIN, TOK), bf),
            pltpu.VMEM((EXPERTS * WIN, 128), jnp.float32),
            pltpu.SemaphoreType.DMA((5, C)),
            pltpu.SemaphoreType.DMA((5, C)),
            pltpu.SemaphoreType.DMA((4,)),
            pltpu.SemaphoreType.DMA((2,)),
        ],
        compiler_params=pltpu.CompilerParams(
            collective_id=0, has_side_effects=True, vmem_limit_bytes=62 * 2**20
        ),
        cost_estimate=pl.CostEstimate(
            flops=4 * ROWS * D * FFD, bytes_accessed=2 * (2 * ROWS * FFD + 2 * FFD * D), transcendentals=0
        ),
    )(routes.T, probs.T, grad_out, rows_hidden, w_down)


def solution(mesh):
    return jax.shard_map(
        per_device,
        mesh=mesh,
        in_specs=(
            P(("rep", "exp"), None),
            P(("rep", "exp"), None),
            P(("rep", "exp"), None),
            P("exp", None, "rep"),
            P("exp", "rep", None),
        ),
        out_specs=(P("exp", None, "rep"), P("exp", "rep", None)),
        check_vma=False,
    )
```

time: 276 us -> 124 us (0.45)
  waiting for transfers between devices: 138 us -> 0 us
  Pallas kernels: 0 us -> 116 us
  matrix products: 40.9 us -> 0 us
  local copies, waits for them, and re-layouts: 41.8 us -> 6.66 us
  blocking collectives: 33.8 us -> 0 us
  between operations: 14.1 us -> 0.65 us
  other arithmetic: 7.1 us -> 0 us
    all_gather x1 -> x0, waiting for transfers between devices: 138 us -> none  [per_device(): piece = lax.all_gather(own_cot, 'rep', axis=0, tiled=True)]
    pallas_call x0 -> x1, Pallas kernels: none -> 116 us  [per_device(): pl.pallas_call(gather_kernel, out_shape=(jax.ShapeDtypeStruct((1, ROWS, F...]
    dot_general x2 -> x0, matrix products: 40.9 us -> none  [the longest x1 21.8 us: per_device(): jnp.einsum('lnch,nlcd->lhd', hidden_blocks, piece, preferred_element_type...]
    all_to_all x1 -> x0, blocking collectives: 33.8 us -> none  [per_device(): lax.all_to_all(send_cot, 'exp', split_axis=0, concat_axis=0, tiled=True)]
    reshape x2 -> x0, local copies, waits for them, and re-layouts: 10.5 us -> none  [the longest x1 7.9 us: per_device(): d_rows = d_all.reshape(owned, block_count * CAP, hid_width)]
    convert_element_type x2 -> x0, local copies, waits for them, and re-layouts: 10.4 us -> none  [the longest x1 5.22 us: per_device(): jnp.repeat(grad_out, 2, axis=0).astype(jnp.float32)]
    another operation x2 -> x0, local copies, waits for them, and re-layouts: 7.89 us -> none
    scatter x1 -> x0, other arithmetic: 5.54 us -> none  [per_device(): jnp.zeros((experts * CAP, model_width), jnp.bfloat16).at[target].set(scaled)]
  transfers between devices with their start and end apart: 1 -> 0, of which waited for: 1 -> 0; matrix products, arithmetic and copies ran while one was open for 3% -> 0% of each run, Pallas kernels for 0% -> 0%
where the time goes in v1:
time: 124 us
  Pallas kernels  116 us (94%)
  local copies, waits for them, and re-layouts  6.66 us (5%)
    pallas_call x1, Pallas kernels, per_device(): pl.pallas_call(gather_kernel, out_shape=(jax.ShapeDtypeStruct((1, ROWS, F...  116 us
    unnamed x4, local copies, waits for them, and re-layouts  6.66 us

profile of v1, /device:TPU:1, one launch (start us, length us, event | category | flops | bytes accessed | tf_op | source)
XLA Modules:
  0.0 123.6 jit_solution(3207441188044949177)
XLA Ops:
  0.6 116.3 %shard_map.68 = (bf16[1,4608,512]{2,1,0:T(8,128)(2,1)}, bf16[1,512,3072]{2,1,0:T(8,128)(2,1)}) custom-call(s32[2,128]{1,0:T(2,128)} %bitcast.2, f32[2,128]{1,0:T(2,128)} %bitcast.3, bf16[128,3072]{1,0:T(8,128)(2,1)} %g_hbm.1, bf16[1,4608,512]{2,1,0:T(8,128)(2,1)} %h_hbm.1, bf16[1,512,3072]{2,1,0:T(8,128)(2,1)} %w_hbm.1), custom_call_target="tpu_custom_call" | custom-call | flops 28991029248 | bytes 15728640 | tf_op jit(solution)/shard_map/pallas_call | solution.py:283
  117.0 0.0 copy-start
  117.0 5.0 %copy.9 = bf16[1,4608,512]{2,1,0:T(8,128)(2,1)} copy(bf16[1,4608,512]{2,1,0:T(8,128)(2,1)} %get-tuple-element.4) | data formatting | bytes 9437184
  122.0 0.0 copy-done
  122.0 1.7 %copy.10 = bf16[1,512,3072]{2,1,0:T(8,128)(2,1)} copy(bf16[1,512,3072]{2,1,0:T(8,128)(2,1)S(1)} %copy-done) | data formatting | bytes 6291456
Async XLA Ops:
  117.0 5.0 %copy-start = (bf16[1,512,3072]{2,1,0:T(8,128)(2,1)S(1)}, bf16[1,512,3072]{2,1,0:T(8,128)(2,1)}, u32[]{:S(2)}) copy-start(bf16[1,512,3072]{2,1,0:T(8,128)(2,1)} %get-tuple-element.5) | copy-start | bytes 9437188

commit v2 on v0

v2 whole, which is shorter than its diff:
```python
import jax
import jax.numpy as jnp
from jax import lax
from jax.experimental import pallas as pl
from jax.experimental.pallas import tpu as pltpu
from jax.sharding import PartitionSpec as P

CAP = 36
EXPERTS = 8
TOK = 128
D = 3072
FFD = 512
ROWS = 4608
LANES = 128
COLS = D // LANES
PAIRS = COLS // 2
NC = PAIRS + 2
WIN = 48
GRP = 4 * CAP
UNIT = 2 * GRP
NU = 16
A = 160
A1 = 64
BR = UNIT - A
MESH = pl.DeviceIdType.MESH

LEXP, L1, L2, L3, LC1, LC2, LC3, LC4 = range(8)
BLK = 4 * UNIT


def gather_kernel(
    rt_ref, pt_ref, g_hbm, h_hbm, w_hbm, d_out, gd_out,
    dy, send, recv, ht, wv, gv, acc, gacc, sel, prow,
    ssem, rsem, lsem,
):
    rep = lax.axis_index("rep")
    ex = lax.axis_index("exp")
    lo, y, core = rep // 8, (rep // 2) % 4, rep % 2
    hi, z = ex // 4, ex % 4
    hb = d_out.at[0]

    def unit(dl, dyy):
        return ((lo + dl) % 2 * 4 + (y + dyy + 4) % 4) * 2 + core

    to_x = (unit(1, 0), ex)
    to_yp = (unit(0, 1), ex)
    to_ym = (unit(0, -1), ex)
    to_core = ((lo * 4 + y) * 2 + 1 - core, ex)
    spread = []
    for dh in range(2):
        for dz in (2, 1, 3, 0):
            if dh or dz:
                hz = (hi + dh) % 2 * 4 + (z + dz) % 4
                spread.append((dh, (unit(dh, 0), hz), hz))
    peers = [to_x, to_yp, to_ym, to_core] + [s[1] for s in spread]

    load_g = pltpu.make_async_copy(g_hbm, gv, lsem.at[0])
    load_w = pltpu.make_async_copy(w_hbm.at[0], wv, lsem.at[1])
    load_g.start()

    bar = pltpu.get_barrier_semaphore()
    for p in peers:
        pl.semaphore_signal(bar, inc=1, device_id=p, device_id_type=MESH)

    def group_rows(i):
        u, part = i // 2, i % 2
        g = (u + 8 * part) % 16 * 2 + (hi + part) % 2
        return pl.ds(pl.multiple_of(g * GRP, 16), GRP)

    def local_rows(i):
        return pl.ds(pl.multiple_of(i * GRP, 16), GRP)

    def start_hidden(i, _):
        pltpu.make_async_copy(
            h_hbm.at[0, group_rows(i)], hb.at[local_rows(i)], lsem.at[2]
        ).start()
        return 0

    rt = rt_ref[...]
    pt = pt_ref[...]
    erow = lax.broadcasted_iota(jnp.int32, (EXPERTS, TOK), 0)
    oh0 = (rt[0:1] == erow).astype(jnp.float32)
    oh1 = (rt[1:2] == erow).astype(jnp.float32)
    upper = (
        lax.broadcasted_iota(jnp.int32, (TOK, TOK), 0)
        < lax.broadcasted_iota(jnp.int32, (TOK, TOK), 1)
    ).astype(jnp.float32)
    before = jnp.dot(oh0 + oh1, upper, preferred_element_type=jnp.float32)
    slot0 = jnp.sum(oh0 * before, axis=0, keepdims=True).astype(jnp.int32)
    slot1 = jnp.sum(oh1 * before, axis=0, keepdims=True).astype(jnp.int32)
    t0 = rt[0:1] * WIN + slot0 + 4 * z
    t1 = rt[1:2] * WIN + slot1 + 4 * z
    row = lax.broadcasted_iota(jnp.int32, (EXPERTS * WIN, TOK), 0)
    m0 = row == t0
    m1 = row == t1
    sel[...] = (m0 | m1).astype(jnp.float32).astype(jnp.bfloat16)
    pw = jnp.where(m0, pt[0:1], 0.0) + jnp.where(m1, pt[1:2], 0.0)
    prow[...] = jnp.broadcast_to(jnp.sum(pw, axis=1, keepdims=True), prow.shape)

    def tile0(c):
        return jnp.where(c < 2, c, jnp.where(c < NC - 2, 2 * c - 2, c + COLS - NC))

    def wide(c, fn):
        one = (c < 2) | (c >= NC - 2)

        @pl.when(one)
        def _():
            fn(c, 1)

        @pl.when(jnp.logical_not(one))
        def _():
            fn(c, 2)

    def remote(src, dst, stage, c, device):
        s = 0 if stage == LEXP else 1
        pltpu.make_async_remote_copy(
            src_ref=src, dst_ref=dst, send_sem=ssem.at[s, c], recv_sem=rsem.at[stage, c],
            device_id=device, device_id_type=MESH,
        ).start()

    def wait_rows(sem, c, n, rows):
        ref = dy.at[pl.ds(tile0(c), n), pl.ds(0, rows)]
        pltpu.make_async_copy(ref, ref, sem).wait()

    def wait_windows(sem, c, n):
        ref = recv.at[pl.ds(tile0(c), n), pl.ds(0, 7)]
        pltpu.make_async_copy(ref, ref, sem).wait()

    def push(stage, c, n, u, start, rows, device):
        ref = dy.at[pl.ds(tile0(c), n), pl.ds(pl.multiple_of(u * UNIT + start, 16), rows)]
        remote(ref, ref, stage, c, device)

    def make_windows(c, n):
        g = gv[:, pl.ds(pl.multiple_of(tile0(c) * LANES, LANES), n * LANES)]
        rows = jnp.dot(sel[...], g, preferred_element_type=jnp.float32)
        for i in range(n):
            tile = rows[:, i * LANES : (i + 1) * LANES] * prow[...]
            send[tile0(c) + i] = tile.astype(jnp.bfloat16)

    def send_windows(c, n):
        for dh, device, e in spread:
            remote(
                send.at[pl.ds(tile0(c), n), pl.ds(pl.multiple_of(e * WIN, 16), WIN)],
                recv.at[pl.ds(tile0(c), n), dh * 4 + z],
                LEXP, c, device,
            )
        for i in range(n):
            recv[tile0(c) + i, z] = send[tile0(c) + i, pl.ds(pl.multiple_of(ex * WIN, 16), WIN), :]

    def prep(c, n):
        make_windows(c, n)
        send_windows(c, n)

    def stage1(c, n):
        wait_windows(rsem.at[LEXP, c], c, n)
        for i in range(n):
            k = tile0(c) + i
            for part in range(2):
                for s in range(4):
                    at = rep * UNIT + part * GRP + s * 32
                    q = part * 4 + s
                    if s == 0:
                        first = recv[k, q, 0:16, :]
                    else:
                        first = recv[k, q - 1, 32:48, :] + recv[k, q, 0:16, :]
                    dy[k, pl.ds(pl.multiple_of(at, 16), 16), :] = first
                    dy[k, pl.ds(pl.multiple_of(at + 16, 16), 16), :] = recv[k, q, 16:32, :]
                    if s == 3:
                        dy[k, pl.ds(pl.multiple_of(at + 32, 16), 16), :] = recv[k, q, 32:48, :]
        for device in (to_x, to_yp, to_ym):
            push(L1, c, n, rep, 0, UNIT, device)
        push(LC1, c, n, rep, 0, UNIT, to_core)

    def stage2(c, n):
        wait_rows(rsem.at[L1, c], c, n, 3 * UNIT)
        push(L2, c, n, unit(0, -1), 0, A, to_yp)
        push(L2, c, n, unit(0, 1), A, BR, to_ym)
        push(L2, c, n, unit(0, 1), A, BR, to_x)
        push(L2, c, n, unit(1, 0), 0, A, to_yp)
        push(L2, c, n, unit(1, 0), 0, A, to_ym)
        push(L2, c, n, unit(0, -1), A, BR, to_x)
        for u in (unit(1, 0), unit(0, 1), unit(0, -1)):
            push(LC2, c, n, u, 0, UNIT, to_core)

    def stage3(c, n):
        wait_rows(rsem.at[L2, c], c, n, 3 * UNIT)
        push(L3, c, n, unit(1, -1), 0, A1, to_yp)
        push(L3, c, n, unit(1, 1), A1, A - A1, to_ym)
        push(L3, c, n, unit(0, 2), A, BR, to_x)
        for u in (unit(0, 2), unit(1, 1), unit(1, -1)):
            push(LC3, c, n, u, 0, UNIT, to_core)

    def stage4(c, n):
        wait_rows(rsem.at[L3, c], c, n, UNIT)
        push(LC4, c, n, unit(1, 2), 0, UNIT, to_core)

    def arrived(c, n):
        wait_rows(rsem.at[LC1, c], c, n, UNIT)
        wait_rows(rsem.at[LC2, c], c, n, 3 * UNIT)
        wait_rows(rsem.at[LC3, c], c, n, 3 * UNIT)
        wait_rows(rsem.at[LC4, c], c, n, UNIT)

    def multiply(k, b):
        at = pl.ds(pl.multiple_of(b * BLK, BLK), BLK)
        rows = jnp.concatenate([dy[2 * k, at, :], dy[2 * k + 1, at, :]], axis=1)
        wc = wv[:, pl.ds(pl.multiple_of(k * 2 * LANES, 2 * LANES), 2 * LANES)]
        gacc[...] += jnp.dot(ht[:, at], rows, preferred_element_type=jnp.float32)
        acc[at, :] += lax.dot_general(
            rows, wc, (((1,), (1,)), ((), ())), preferred_element_type=jnp.float32
        )

    def put_grad(k, grad):
        cols = pl.ds(pl.multiple_of(k * 2 * LANES, 2 * LANES), 2 * LANES)
        gd_out[0, :, cols] = grad.astype(jnp.bfloat16)

    def compute(k):
        rows = jnp.concatenate([dy[2 * k], dy[2 * k + 1]], axis=1)
        wc = wv[:, pl.ds(pl.multiple_of(k * 2 * LANES, 2 * LANES), 2 * LANES)]
        put_grad(k, jnp.dot(ht[...], rows, preferred_element_type=jnp.float32))
        acc[...] += lax.dot_general(
            rows, wc, (((1,), (1,)), ((), ())), preferred_element_type=jnp.float32
        )

    def finish(b):
        multiply(PAIRS - 1, b)

        def body(i, _):
            n = b * (BLK // GRP) + i
            d_out[0, group_rows(n), :] = acc[local_rows(n), :].astype(jnp.bfloat16)
            return 0

        lax.fori_loop(0, BLK // GRP, body, 0)

    def turn_hidden(part):
        def body(i, _):
            at = pl.ds(pl.multiple_of((part * 9 + i) * 128, 128), 128)
            ht[:, at] = hb[at, :].T
            return 0

        lax.fori_loop(0, 9, body, 0)
        at = pl.ds(pl.multiple_of(part * BLK, BLK), BLK)
        acc[at, :] = jnp.zeros((BLK, FFD), jnp.float32)

    load_g.wait()
    make_windows(0, 1)
    pl.semaphore_wait(bar, len(peers))
    send_windows(0, 1)
    lax.fori_loop(0, 32, start_hidden, 0)
    load_w.start()
    prep(1, 1)
    make_windows(2, 2)

    def step(t, _):
        def stage(lag, fn):
            c = t - lag

            @pl.when((c >= 0) & (c < NC))
            def _():
                wide(c, fn)

        stage(0, stage1)

        @pl.when(t == 0)
        def _():
            send_windows(2, 2)

        stage(1, stage2)
        stage(2, stage3)
        stage(3, stage4)

        @pl.when((t > 0) & (t + 2 < NC))
        def _():
            wide(t + 2, prep)

        @pl.when(t == 0)
        def _():
            pltpu.make_async_copy(hb, hb, lsem.at[2]).wait()
            load_w.wait()

        @pl.when(t < 4)
        def _():
            turn_hidden(t)

        stage(3, arrived)

        @pl.when((t >= 4) & (t < PAIRS + 3))
        def _():
            compute(t - 4)

        return 0

    lax.fori_loop(0, NC + 2, step, 0)

    last = NC - 1
    gacc[...] = jnp.zeros_like(gacc)
    wait_rows(rsem.at[LC1, last], last, 1, UNIT)
    wait_rows(rsem.at[LC2, last], last, 1, 3 * UNIT)
    wait_rows(rsem.at[LC3, last], last, 1, 3 * UNIT)
    late = (1 - lo) * 2 + (y + 2) % 4 // 2

    def tail(i, _):
        @pl.when(i == 2)
        def _():
            stage4(last, 1)

        @pl.when(i == 3)
        def _():
            wait_rows(rsem.at[LC4, last], last, 1, UNIT)

        finish((late + 1 + i) % 4)
        return 0

    lax.fori_loop(0, 4, tail, 0)
    put_grad(PAIRS - 1, gacc[...])

    def drain(c, _):
        def one(c, n):
            wait_windows(ssem.at[0, c], c, n)
            wait_rows(ssem.at[1, c], c, n, 15 * UNIT)

        wide(c, one)
        return 0

    lax.fori_loop(0, NC, drain, 0)


def store_kernel(d_in, gd_in, d_hbm, gd_hbm, sem):
    d = pltpu.make_async_copy(d_in, d_hbm, sem.at[0])
    g = pltpu.make_async_copy(gd_in, gd_hbm, sem.at[1])
    d.start()
    g.start()
    d.wait()
    g.wait()


def per_device(grad_out, routes, probs, rows_hidden, w_down):
    bf = jnp.bfloat16
    any_spec = pl.BlockSpec(memory_space=pl.ANY)
    vmem = pl.BlockSpec(memory_space=pltpu.VMEM)
    d_shape, gd_shape = (1, ROWS, FFD), (1, FFD, D)
    d_rows, grad = pl.pallas_call(
        gather_kernel,
        out_shape=(pltpu.VMEM(d_shape, bf), pltpu.VMEM(gd_shape, bf)),
        in_specs=[vmem, vmem, any_spec, any_spec, any_spec],
        out_specs=(vmem, vmem),
        scratch_shapes=[
            pltpu.VMEM((COLS, ROWS, LANES), bf),
            pltpu.VMEM((COLS, EXPERTS * WIN, LANES), bf),
            pltpu.VMEM((COLS, 8, WIN, LANES), bf),
            pltpu.VMEM((FFD, ROWS), bf),
            pltpu.VMEM((FFD, D), bf),
            pltpu.VMEM((TOK, D), bf),
            pltpu.VMEM((ROWS, FFD), jnp.float32),
            pltpu.VMEM((FFD, 2 * LANES), jnp.float32),
            pltpu.VMEM((EXPERTS * WIN, TOK), bf),
            pltpu.VMEM((EXPERTS * WIN, LANES), jnp.float32),
            pltpu.SemaphoreType.DMA((2, NC)),
            pltpu.SemaphoreType.DMA((8, NC)),
            pltpu.SemaphoreType.DMA((3,)),
        ],
        compiler_params=pltpu.CompilerParams(
            collective_id=0, has_side_effects=True, vmem_limit_bytes=54 * 2**20
        ),
        cost_estimate=pl.CostEstimate(
            flops=4 * ROWS * D * FFD, bytes_accessed=2 * (2 * ROWS * FFD + 2 * FFD * D), transcendentals=0
        ),
    )(routes.T, probs.T, grad_out, rows_hidden, w_down)
    return pl.pallas_call(
        store_kernel,
        out_shape=(jax.ShapeDtypeStruct(d_shape, bf), jax.ShapeDtypeStruct(gd_shape, bf)),
        in_specs=[vmem, vmem],
        out_specs=(any_spec, any_spec),
        scratch_shapes=[pltpu.SemaphoreType.DMA((2,))],
        compiler_params=pltpu.CompilerParams(vmem_limit_bytes=2 * 2**20),
    )(
        pltpu.with_memory_space_constraint(d_rows, pltpu.VMEM),
        pltpu.with_memory_space_constraint(grad, pltpu.VMEM),
    )


def solution(mesh):
    return jax.shard_map(
        per_device,
        mesh=mesh,
        in_specs=(
            P(("rep", "exp"), None),
            P(("rep", "exp"), None),
            P(("rep", "exp"), None),
            P("exp", None, "rep"),
            P("exp", "rep", None),
        ),
        out_specs=(P("exp", None, "rep"), P("exp", "rep", None)),
        check_vma=False,
    )
```

time: 276 us -> 118 us (0.43)
  waiting for transfers between devices: 138 us -> 0 us
  Pallas kernels: 0 us -> 117 us
  local copies, waits for them, and re-layouts: 41.8 us -> 0 us
  matrix products: 40.9 us -> 0 us
  blocking collectives: 33.8 us -> 0 us
  between operations: 14.1 us -> 0.64 us
  other arithmetic: 7.1 us -> 0 us
    all_gather x1 -> x0, waiting for transfers between devices: 138 us -> none  [per_device(): piece = lax.all_gather(own_cot, 'rep', axis=0, tiled=True)]
    pallas_call x0 -> x2, Pallas kernels: none -> 117 us  [the longest x1 114 us: per_device(): pl.pallas_call(gather_kernel, out_shape=(pltpu.VMEM(d_shape, bf), pltpu.V...]
    dot_general x2 -> x0, matrix products: 40.9 us -> none  [the longest x1 21.8 us: per_device(): jnp.einsum('lnch,nlcd->lhd', hidden_blocks, piece, preferred_element_type...]
    all_to_all x1 -> x0, blocking collectives: 33.8 us -> none  [per_device(): lax.all_to_all(send_cot, 'exp', split_axis=0, concat_axis=0, tiled=True)]
    reshape x2 -> x0, local copies, waits for them, and re-layouts: 10.5 us -> none  [the longest x1 7.9 us: per_device(): d_rows = d_all.reshape(owned, block_count * CAP, hid_width)]
    convert_element_type x2 -> x0, local copies, waits for them, and re-layouts: 10.4 us -> none  [the longest x1 5.22 us: per_device(): jnp.repeat(grad_out, 2, axis=0).astype(jnp.float32)]
    another operation x2 -> x0, local copies, waits for them, and re-layouts: 7.89 us -> none
    unnamed x7 -> x0, local copies, waits for them, and re-layouts: 6.3 us -> none
  transfers between devices with their start and end apart: 1 -> 0, of which waited for: 1 -> 0; matrix products, arithmetic and copies ran while one was open for 3% -> 0% of each run, Pallas kernels for 0% -> 0%
where the time goes in v2:
time: 118 us; the launch traced here: 117 us
  Pallas kernels  117 us (99%)
    pallas_call x1, Pallas kernels, per_device(): pl.pallas_call(gather_kernel, out_shape=(pltpu.VMEM(d_shape, bf), pltpu.V...  114 us
    pallas_call x1, Pallas kernels, per_device(): pl.pallas_call(store_kernel, out_shape=(jax.ShapeDtypeStruct(d_shape, bf)...  3.24 us

profile of v2, /device:TPU:1, one launch (start us, length us, event | category | flops | bytes accessed | tf_op | source)
XLA Modules:
  0.0 117.4 jit_solution(5763321715704315206)
XLA Ops:
  0.6 113.5 %shard_map.68 = (bf16[1,4608,512]{2,1,0:T(8,128)(2,1)S(1)}, bf16[1,512,3072]{2,1,0:T(8,128)(2,1)S(1)}) custom-call(s32[2,128]{1,0:T(2,128)} %bitcast.2, f32[2,128]{1,0:T(2,128)} %bitcast.3, bf16[128,3072]{1,0:T(8,128)(2,1)} %g_hbm.1, bf16[1,4608,512]{2,1,0:T(8,128)(2,1)} %h_hbm.1, bf16[1,512,3072]{2,1,0:T(8,128)(2,1)} %w_hbm.1), custom_call_target="tpu_custom_call" | custom-call | flops 28991029248 | bytes 15728640 | tf_op jit(solution)/shard_map/pallas_call | solution.py:341
  114.1 3.2 %shard_map.69 = (bf16[1,4608,512]{2,1,0:T(8,128)(2,1)}, bf16[1,512,3072]{2,1,0:T(8,128)(2,1)}) custom-call(bf16[1,4608,512]{2,1,0:T(8,128)(2,1)S(1)} %get-tuple-element.4.d_in, bf16[1,512,3072]{2,1,0:T(8,128)(2,1)S(1)} %get-tuple-element.5.gd_in), custom_call_target="tpu_custom_call" | custom-call | tf_op jit(solution)/shard_map/pallas_call | solution.py:368

commit v3 on v2

--- a/solution.py
+++ b/solution.py
@@ -14,7 +14,8 @@
 LANES = 128
 COLS = D // LANES
 PAIRS = COLS // 2
-NC = PAIRS + 2
+HEAD, TAIL = 2, 2
+NC = HEAD + (COLS - HEAD - TAIL) // 2 + TAIL
 WIN = 48
 GRP = 4 * CAP
 UNIT = 2 * GRP
@@ -29,8 +30,8 @@
 
 
 def gather_kernel(
-    rt_ref, pt_ref, g_hbm, h_hbm, w_hbm, d_out, gd_out,
-    dy, send, recv, ht, wv, gv, acc, gacc, sel, prow,
+    rt_hbm, pt_hbm, g_hbm, h_hbm, w_hbm, d_out, gd_out,
+    rt_ref, pt_ref, dy, send, recv, ht, wv, gv, acc, gacc, sel, prow,
     ssem, rsem, lsem,
 ):
     rep = lax.axis_index("rep")
@@ -56,6 +57,10 @@
 
     load_g = pltpu.make_async_copy(g_hbm, gv, lsem.at[0])
     load_w = pltpu.make_async_copy(w_hbm.at[0], wv, lsem.at[1])
+    load_r = pltpu.make_async_copy(rt_hbm, rt_ref, lsem.at[3])
+    load_p = pltpu.make_async_copy(pt_hbm, pt_ref, lsem.at[4])
+    load_r.start()
+    load_p.start()
     load_g.start()
 
     bar = pltpu.get_barrier_semaphore()
@@ -76,6 +81,8 @@
         ).start()
         return 0
 
+    load_r.wait()
+    load_p.wait()
     rt = rt_ref[...]
     pt = pt_ref[...]
     erow = lax.broadcasted_iota(jnp.int32, (EXPERTS, TOK), 0)
@@ -98,10 +105,10 @@
     prow[...] = jnp.broadcast_to(jnp.sum(pw, axis=1, keepdims=True), prow.shape)
 
     def tile0(c):
-        return jnp.where(c < 2, c, jnp.where(c < NC - 2, 2 * c - 2, c + COLS - NC))
+        return jnp.where(c < HEAD, c, jnp.where(c < NC - TAIL, 2 * c - HEAD, c + COLS - NC))
 
     def wide(c, fn):
-        one = (c < 2) | (c >= NC - 2)
+        one = (c < HEAD) | (c >= NC - TAIL)
 
         @pl.when(one)
         def _():
@@ -198,38 +205,68 @@
         wait_rows(rsem.at[LC1, c], c, n, UNIT)
         wait_rows(rsem.at[LC2, c], c, n, 3 * UNIT)
         wait_rows(rsem.at[LC3, c], c, n, 3 * UNIT)
-        wait_rows(rsem.at[LC4, c], c, n, UNIT)
 
     def multiply(k, b):
         at = pl.ds(pl.multiple_of(b * BLK, BLK), BLK)
         rows = jnp.concatenate([dy[2 * k, at, :], dy[2 * k + 1, at, :]], axis=1)
         wc = wv[:, pl.ds(pl.multiple_of(k * 2 * LANES, 2 * LANES), 2 * LANES)]
-        gacc[...] += jnp.dot(ht[:, at], rows, preferred_element_type=jnp.float32)
+        gacc[k % 2] += jnp.dot(ht[:, at], rows, preferred_element_type=jnp.float32)
         acc[at, :] += lax.dot_general(
             rows, wc, (((1,), (1,)), ((), ())), preferred_element_type=jnp.float32
         )
 
-    def put_grad(k, grad):
-        cols = pl.ds(pl.multiple_of(k * 2 * LANES, 2 * LANES), 2 * LANES)
-        gd_out[0, :, cols] = grad.astype(jnp.bfloat16)
-
-    def compute(k):
-        rows = jnp.concatenate([dy[2 * k], dy[2 * k + 1]], axis=1)
-        wc = wv[:, pl.ds(pl.multiple_of(k * 2 * LANES, 2 * LANES), 2 * LANES)]
-        put_grad(k, jnp.dot(ht[...], rows, preferred_element_type=jnp.float32))
-        acc[...] += lax.dot_general(
-            rows, wc, (((1,), (1,)), ((), ())), preferred_element_type=jnp.float32
-        )
-
-    def finish(b):
-        multiply(PAIRS - 1, b)
-
+    def flush(b):
         def body(i, _):
             n = b * (BLK // GRP) + i
             d_out[0, group_rows(n), :] = acc[local_rows(n), :].astype(jnp.bfloat16)
             return 0
 
         lax.fori_loop(0, BLK // GRP, body, 0)
+
+    late_block = (1 - lo) * 2 + (y + 2) % 4 // 2
+
+    def completes(c):
+        wide_c = (c >= HEAD) & (c < NC - TAIL)
+        return (c >= 0) & (c < NC) & (wide_c | (tile0(c) % 2 == 1))
+
+    def early(c):
+        k = tile0(c) // 2
+        gacc[k % 2] = jnp.zeros(gacc.shape[1:], jnp.float32)
+
+        def body(i, _):
+            if TAIL:
+
+                @pl.when((c == NC - 1) & (i == 2))
+                def _():
+                    stage4(NC - 1, 1)
+
+                @pl.when((c == NC - 3) & (i == 1))
+                def _():
+                    stage2(NC - 1, 1)
+
+            b = (late_block + 1 + i) % 4
+            multiply(k, b)
+
+            @pl.when(k == PAIRS - 1)
+            def _():
+                flush(b)
+
+            return 0
+
+        lax.fori_loop(0, 3, body, 0)
+
+    def late(c, n):
+        if n == 1:
+            wait_rows(rsem.at[LC4, c - 1], c - 1, 1, UNIT)
+        wait_rows(rsem.at[LC4, c], c, n, UNIT)
+        k = tile0(c) // 2
+        multiply(k, late_block)
+        cols = pl.ds(pl.multiple_of(k * 2 * LANES, 2 * LANES), 2 * LANES)
+        gd_out[0, :, cols] = gacc[k % 2].astype(jnp.bfloat16)
+
+        @pl.when(k == PAIRS - 1)
+        def _():
+            flush(late_block)
 
     def turn_hidden(part):
         def body(i, _):
@@ -251,10 +288,10 @@
     make_windows(2, 2)
 
     def step(t, _):
-        def stage(lag, fn):
+        def stage(lag, fn, but=0):
             c = t - lag
 
-            @pl.when((c >= 0) & (c < NC))
+            @pl.when((c >= 0) & (c < NC - but))
             def _():
                 wide(c, fn)
 
@@ -264,13 +301,23 @@
         def _():
             send_windows(2, 2)
 
-        stage(1, stage2)
+
+        @pl.when((t > 0) & (t + 2 < NC))
+        def _():
+            wide(t + 2, prep)
+
+        stage(1, stage2, 1)
+
+        @pl.when(completes(t - 4) & (t < NC))
+        def _():
+            wide(t - 4, late)
+
         stage(2, stage3)
-        stage(3, stage4)
-
-        @pl.when((t > 0) & (t + 2 < NC))
-        def _():
-            wide(t + 2, prep)
+        stage(3, stage4, 1)
+
+        @pl.when(completes(t - 4) & (t >= NC))
+        def _():
+            wide(t - 4, late)
 
         @pl.when(t == 0)
         def _():
@@ -281,37 +328,15 @@
         def _():
             turn_hidden(t)
 
-        stage(3, arrived)
-
-        @pl.when((t >= 4) & (t < PAIRS + 3))
-        def _():
-            compute(t - 4)
+        stage(2, arrived)
+
+        @pl.when(completes(t - 2))
+        def _():
+            early(t - 2)
 
         return 0
 
-    lax.fori_loop(0, NC + 2, step, 0)
-
-    last = NC - 1
-    gacc[...] = jnp.zeros_like(gacc)
-    wait_rows(rsem.at[LC1, last], last, 1, UNIT)
-    wait_rows(rsem.at[LC2, last], last, 1, 3 * UNIT)
-    wait_rows(rsem.at[LC3, last], last, 1, 3 * UNIT)
-    late = (1 - lo) * 2 + (y + 2) % 4 // 2
-
-    def tail(i, _):
-        @pl.when(i == 2)
-        def _():
-            stage4(last, 1)
-
-        @pl.when(i == 3)
-        def _():
-            wait_rows(rsem.at[LC4, last], last, 1, UNIT)
-
-        finish((late + 1 + i) % 4)
-        return 0
-
-    lax.fori_loop(0, 4, tail, 0)
-    put_grad(PAIRS - 1, gacc[...])
+    lax.fori_loop(0, NC + 4, step, 0)
 
     def drain(c, _):
         def one(c, n):
@@ -341,9 +366,11 @@
     d_rows, grad = pl.pallas_call(
         gather_kernel,
         out_shape=(pltpu.VMEM(d_shape, bf), pltpu.VMEM(gd_shape, bf)),
-        in_specs=[vmem, vmem, any_spec, any_spec, any_spec],
+        in_specs=[any_spec] * 5,
         out_specs=(vmem, vmem),
         scratch_shapes=[
+            pltpu.VMEM((2, TOK), jnp.int32),
+            pltpu.VMEM((2, TOK), jnp.float32),
             pltpu.VMEM((COLS, ROWS, LANES), bf),
             pltpu.VMEM((COLS, EXPERTS * WIN, LANES), bf),
             pltpu.VMEM((COLS, 8, WIN, LANES), bf),
@@ -351,12 +378,12 @@
             pltpu.VMEM((FFD, D), bf),
             pltpu.VMEM((TOK, D), bf),
             pltpu.VMEM((ROWS, FFD), jnp.float32),
-            pltpu.VMEM((FFD, 2 * LANES), jnp.float32),
+            pltpu.VMEM((2, FFD, 2 * LANES), jnp.float32),
             pltpu.VMEM((EXPERTS * WIN, TOK), bf),
             pltpu.VMEM((EXPERTS * WIN, LANES), jnp.float32),
             pltpu.SemaphoreType.DMA((2, NC)),
             pltpu.SemaphoreType.DMA((8, NC)),
-            pltpu.SemaphoreType.DMA((3,)),
+            pltpu.SemaphoreType.DMA((5,)),
         ],
         compiler_params=pltpu.CompilerParams(
             collective_id=0, has_side_effects=True, vmem_limit_bytes=54 * 2**20

time: 118 us -> 115 us (0.975)
  Pallas kernels: 117 us -> 115 us
    pallas_call x1, Pallas kernels: 114 us -> 111 us  [per_device(): pl.pallas_call(gather_kernel, out_shape=(pltpu.VMEM(d_shape, bf), pltpu.V...]
where the time goes in v3:
time: 115 us
  Pallas kernels  115 us (100%)
    pallas_call x1, Pallas kernels, per_device(): pl.pallas_call(gather_kernel, out_shape=(pltpu.VMEM(d_shape, bf), pltpu.V...  111 us
    pallas_call x1, Pallas kernels, per_device(): pl.pallas_call(store_kernel, out_shape=(jax.ShapeDtypeStruct(d_shape, bf)...  3.24 us

profile of v3, /device:TPU:1, one launch (start us, length us, event | category | flops | bytes accessed | tf_op | source)
XLA Modules:
  0.0 115.3 jit_solution(18302033708173543141)
XLA Ops:
  0.6 111.4 %shard_map.68 = (bf16[1,4608,512]{2,1,0:T(8,128)(2,1)S(1)}, bf16[1,512,3072]{2,1,0:T(8,128)(2,1)S(1)}) custom-call(s32[2,128]{1,0:T(2,128)} %bitcast.2, f32[2,128]{1,0:T(2,128)} %bitcast.3, bf16[128,3072]{1,0:T(8,128)(2,1)} %g_hbm.1, bf16[1,4608,512]{2,1,0:T(8,128)(2,1)} %h_hbm.1, bf16[1,512,3072]{2,1,0:T(8,128)(2,1)} %w_hbm.1), custom_call_target="tpu_custom_call" | custom-call | flops 28991029248 | bytes 15728640 | tf_op jit(solution)/shard_map/pallas_call | solution.py:366
  112.0 3.2 %shard_map.69 = (bf16[1,4608,512]{2,1,0:T(8,128)(2,1)}, bf16[1,512,3072]{2,1,0:T(8,128)(2,1)}) custom-call(bf16[1,4608,512]{2,1,0:T(8,128)(2,1)S(1)} %get-tuple-element.4.d_in, bf16[1,512,3072]{2,1,0:T(8,128)(2,1)S(1)} %get-tuple-element.5.gd_in), custom_call_target="tpu_custom_call" | custom-call | tf_op jit(solution)/shard_map/pallas_call | solution.py:395

commit v4 on v3

--- a/solution.py
+++ b/solution.py
@@ -27,18 +27,36 @@
 
 LEXP, L1, L2, L3, LC1, LC2, LC3, LC4 = range(8)
 BLK = 4 * UNIT
+DONE = 2
+
+
+def group_rows(hi, i):
+    u, part = i // 2, i % 2
+    g = (u + 8 * part) % 16 * 2 + (hi + part) % 2
+    return pl.ds(pl.multiple_of(g * GRP, 16), GRP)
+
+
+def local_rows(i):
+    return pl.ds(pl.multiple_of(i * GRP, 16), GRP)
+
+
+def block_rows(b):
+    return pl.ds(pl.multiple_of(b * BLK, BLK), BLK)
+
+
+def late_block(lo, y):
+    return (1 - lo) * 2 + (y + 2) % 4 // 2
 
 
 def gather_kernel(
-    rt_hbm, pt_hbm, g_hbm, h_hbm, w_hbm, d_out, gd_out,
-    rt_ref, pt_ref, dy, send, recv, ht, wv, gv, acc, gacc, sel, prow,
+    rt_hbm, pt_hbm, g_hbm, h_hbm, w_hbm, rows_out, acc, gacc, grad, ht, wv,
+    rt_ref, pt_ref, dy, send, recv, hb, gv, sel, prow,
     ssem, rsem, lsem,
 ):
     rep = lax.axis_index("rep")
     ex = lax.axis_index("exp")
     lo, y, core = rep // 8, (rep // 2) % 4, rep % 2
     hi, z = ex // 4, ex % 4
-    hb = d_out.at[0]
 
     def unit(dl, dyy):
         return ((lo + dl) % 2 * 4 + (y + dyy + 4) % 4) * 2 + core
@@ -48,7 +66,7 @@
     to_ym = (unit(0, -1), ex)
     to_core = ((lo * 4 + y) * 2 + 1 - core, ex)
     spread = []
-    for dh in range(2):
+    for dh in (1, 0):
         for dz in (2, 1, 3, 0):
             if dh or dz:
                 hz = (hi + dh) % 2 * 4 + (z + dz) % 4
@@ -67,17 +85,9 @@
     for p in peers:
         pl.semaphore_signal(bar, inc=1, device_id=p, device_id_type=MESH)
 
-    def group_rows(i):
-        u, part = i // 2, i % 2
-        g = (u + 8 * part) % 16 * 2 + (hi + part) % 2
-        return pl.ds(pl.multiple_of(g * GRP, 16), GRP)
-
-    def local_rows(i):
-        return pl.ds(pl.multiple_of(i * GRP, 16), GRP)
-
     def start_hidden(i, _):
         pltpu.make_async_copy(
-            h_hbm.at[0, group_rows(i)], hb.at[local_rows(i)], lsem.at[2]
+            h_hbm.at[0, group_rows(hi, i)], hb.at[local_rows(i)], lsem.at[2]
         ).start()
         return 0
 
@@ -215,15 +225,7 @@
             rows, wc, (((1,), (1,)), ((), ())), preferred_element_type=jnp.float32
         )
 
-    def flush(b):
-        def body(i, _):
-            n = b * (BLK // GRP) + i
-            d_out[0, group_rows(n), :] = acc[local_rows(n), :].astype(jnp.bfloat16)
-            return 0
-
-        lax.fori_loop(0, BLK // GRP, body, 0)
-
-    late_block = (1 - lo) * 2 + (y + 2) % 4 // 2
+    late = late_block(lo, y)
 
     def completes(c):
         wide_c = (c >= HEAD) & (c < NC - TAIL)
@@ -234,39 +236,23 @@
         gacc[k % 2] = jnp.zeros(gacc.shape[1:], jnp.float32)
 
         def body(i, _):
-            if TAIL:
-
-                @pl.when((c == NC - 1) & (i == 2))
-                def _():
-                    stage4(NC - 1, 1)
-
-                @pl.when((c == NC - 3) & (i == 1))
-                def _():
-                    stage2(NC - 1, 1)
-
-            b = (late_block + 1 + i) % 4
-            multiply(k, b)
-
-            @pl.when(k == PAIRS - 1)
+            @pl.when((c == NC - 3) & (i == 1))
             def _():
-                flush(b)
-
+                stage2(NC - 1, 1)
+
+            multiply(k, (late + 1 + i) % 4)
             return 0
 
-        lax.fori_loop(0, 3, body, 0)
-
-    def late(c, n):
+        lax.fori_loop(0, jnp.where(c == NC - 1, DONE, 3), body, 0)
+
+    def finish(c, n):
         if n == 1:
             wait_rows(rsem.at[LC4, c - 1], c - 1, 1, UNIT)
         wait_rows(rsem.at[LC4, c], c, n, UNIT)
         k = tile0(c) // 2
-        multiply(k, late_block)
+        multiply(k, late)
         cols = pl.ds(pl.multiple_of(k * 2 * LANES, 2 * LANES), 2 * LANES)
-        gd_out[0, :, cols] = gacc[k % 2].astype(jnp.bfloat16)
-
-        @pl.when(k == PAIRS - 1)
-        def _():
-            flush(late_block)
+        grad[:, cols] = gacc[k % 2].astype(jnp.bfloat16)
 
     def turn_hidden(part):
         def body(i, _):
@@ -310,14 +296,14 @@
 
         @pl.when(completes(t - 4) & (t < NC))
         def _():
-            wide(t - 4, late)
+            wide(t - 4, finish)
 
         stage(2, stage3)
+        @pl.when(completes(t - 4) & (t >= NC))
+        def _():
+            wide(t - 4, finish)
+
         stage(3, stage4, 1)
-
-        @pl.when(completes(t - 4) & (t >= NC))
-        def _():
-            wide(t - 4, late)
 
         @pl.when(t == 0)
         def _():
@@ -336,7 +322,17 @@
 
         return 0
 
-    lax.fori_loop(0, NC + 4, step, 0)
+    lax.fori_loop(0, NC + 2, step, 0)
+    stage4(NC - 1, 1)
+    for i in range(DONE, 4):
+        if i == 3:
+            for c in (NC - 2, NC - 1):
+                wait_rows(rsem.at[LC4, c], c, 1, UNIT)
+        at = block_rows((late + 1 + i) % 4)
+        for k in range(2):
+            rows_out[(i - DONE) * BLK : (i - DONE + 1) * BLK, k * LANES : (k + 1) * LANES] = dy[
+                COLS - 2 + k, at, :
+            ]
 
     def drain(c, _):
         def one(c, n):
@@ -349,36 +345,74 @@
     lax.fori_loop(0, NC, drain, 0)
 
 
-def store_kernel(d_in, gd_in, d_hbm, gd_hbm, sem):
-    d = pltpu.make_async_copy(d_in, d_hbm, sem.at[0])
-    g = pltpu.make_async_copy(gd_in, gd_hbm, sem.at[1])
-    d.start()
-    g.start()
-    d.wait()
-    g.wait()
+def store_kernel(rows_in, acc, gacc, grad, ht, wv, d_hbm, gd_hbm, d_buf, g_buf, g_sum, sem):
+    rep, ex = lax.axis_index("rep"), lax.axis_index("exp")
+    late, hi = late_block(rep // 8, (rep // 2) % 4), ex // 4
+    last = (PAIRS - 1) * 2 * LANES
+    first = pltpu.make_async_copy(grad.at[:, pl.ds(0, last)], gd_hbm.at[0, :, pl.ds(0, last)], sem.at[0])
+    first.start()
+    g_sum[...] = gacc[(PAIRS - 1) % 2]
+
+    def body(i, _):
+        b = (late + 1 + i) % 4
+        at = block_rows(b)
+
+        @pl.when(i < DONE)
+        def _():
+            d_buf[at, :] = acc[at, :].astype(jnp.bfloat16)
+
+        @pl.when(i >= DONE)
+        def _():
+            rows = rows_in[block_rows(i - DONE), :]
+            part = lax.dot_general(
+                rows, wv[:, last:], (((1,), (1,)), ((), ())), preferred_element_type=jnp.float32
+            )
+            d_buf[at, :] = (acc[at, :] + part).astype(jnp.bfloat16)
+            g_sum[...] += jnp.dot(ht[:, at], rows, preferred_element_type=jnp.float32)
+
+        def put(k, _):
+            n = b * (BLK // GRP) + k
+            pltpu.make_async_copy(
+                d_buf.at[local_rows(n)], d_hbm.at[0, group_rows(hi, n)], sem.at[1]
+            ).start()
+            return 0
+
+        lax.fori_loop(0, BLK // GRP, put, 0)
+        return 0
+
+    lax.fori_loop(0, 4, body, 0)
+    g_buf[...] = g_sum[...].astype(jnp.bfloat16)
+    second = pltpu.make_async_copy(g_buf, gd_hbm.at[0, :, pl.ds(last, 2 * LANES)], sem.at[2])
+    second.start()
+    first.wait()
+    pltpu.make_async_copy(d_buf, d_hbm.at[0], sem.at[1]).wait()
+    second.wait()
 
 
 def per_device(grad_out, routes, probs, rows_hidden, w_down):
     bf = jnp.bfloat16
     any_spec = pl.BlockSpec(memory_space=pl.ANY)
     vmem = pl.BlockSpec(memory_space=pltpu.VMEM)
-    d_shape, gd_shape = (1, ROWS, FFD), (1, FFD, D)
-    d_rows, grad = pl.pallas_call(
+    kept = pl.pallas_call(
         gather_kernel,
-        out_shape=(pltpu.VMEM(d_shape, bf), pltpu.VMEM(gd_shape, bf)),
+        out_shape=(
+            pltpu.VMEM(((4 - DONE) * BLK, 2 * LANES), bf),
+            pltpu.VMEM((ROWS, FFD), jnp.float32),
+            pltpu.VMEM((2, FFD, 2 * LANES), jnp.float32),
+            pltpu.VMEM((FFD, D), bf),
+            pltpu.VMEM((FFD, ROWS), bf),
+            pltpu.VMEM((FFD, D), bf),
+        ),
         in_specs=[any_spec] * 5,
-        out_specs=(vmem, vmem),
+        out_specs=[vmem] * 6,
         scratch_shapes=[
             pltpu.VMEM((2, TOK), jnp.int32),
             pltpu.VMEM((2, TOK), jnp.float32),
             pltpu.VMEM((COLS, ROWS, LANES), bf),
             pltpu.VMEM((COLS, EXPERTS * WIN, LANES), bf),
             pltpu.VMEM((COLS, 8, WIN, LANES), bf),
-            pltpu.VMEM((FFD, ROWS), bf),
-            pltpu.VMEM((FFD, D), bf),
+            pltpu.VMEM((ROWS, FFD), bf),
             pltpu.VMEM((TOK, D), bf),
-            pltpu.VMEM((ROWS, FFD), jnp.float32),
-            pltpu.VMEM((2, FFD, 2 * LANES), jnp.float32),
             pltpu.VMEM((EXPERTS * WIN, TOK), bf),
             pltpu.VMEM((EXPERTS * WIN, LANES), jnp.float32),
             pltpu.SemaphoreType.DMA((2, NC)),
@@ -386,7 +420,7 @@
             pltpu.SemaphoreType.DMA((5,)),
         ],
         compiler_params=pltpu.CompilerParams(
-            collective_id=0, has_side_effects=True, vmem_limit_bytes=54 * 2**20
+            collective_id=0, has_side_effects=True, vmem_limit_bytes=41 * 2**20
         ),
         cost_estimate=pl.CostEstimate(
             flops=4 * ROWS * D * FFD, bytes_accessed=2 * (2 * ROWS * FFD + 2 * FFD * D), transcendentals=0
@@ -394,15 +428,20 @@
     )(routes.T, probs.T, grad_out, rows_hidden, w_down)
     return pl.pallas_call(
         store_kernel,
-        out_shape=(jax.ShapeDtypeStruct(d_shape, bf), jax.ShapeDtypeStruct(gd_shape, bf)),
-        in_specs=[vmem, vmem],
+        out_shape=(
+            jax.ShapeDtypeStruct((1, ROWS, FFD), bf),
+            jax.ShapeDtypeStruct((1, FFD, D), bf),
+        ),
+        in_specs=[vmem] * 6,
         out_specs=(any_spec, any_spec),
-        scratch_shapes=[pltpu.SemaphoreType.DMA((2,))],
-        compiler_params=pltpu.CompilerParams(vmem_limit_bytes=2 * 2**20),
-    )(
-        pltpu.with_memory_space_constraint(d_rows, pltpu.VMEM),
-        pltpu.with_memory_space_constraint(grad, pltpu.VMEM),
-    )
+        scratch_shapes=[
+            pltpu.VMEM((ROWS, FFD), bf),
+            pltpu.VMEM((FFD, 2 * LANES), bf),
+            pltpu.VMEM((FFD, 2 * LANES), jnp.float32),
+            pltpu.SemaphoreType.DMA((3,)),
+        ],
+        compiler_params=pltpu.CompilerParams(vmem_limit_bytes=10 * 2**20),
+    )(*(pltpu.with_memory_space_constraint(a, pltpu.VMEM) for a in kept))
 
 
 def solution(mesh):

time: 115 us -> 114 us (level)
  Pallas kernels: 115 us -> 113 us
    pallas_call x2, Pallas kernels: 115 us -> 113 us  [the longest x1 110 us: per_device(): pl.pallas_call(gather_kernel, out_shape=(pltpu.VMEM(((4 - DONE) * BLK, 2...]
where the time goes in v4:
time: 114 us
  Pallas kernels  113 us (99%)
    pallas_call x1, Pallas kernels, per_device(): pl.pallas_call(gather_kernel, out_shape=(pltpu.VMEM(((4 - DONE) * BLK, 2...  110 us
    pallas_call x1, Pallas kernels, per_device(): pl.pallas_call(store_kernel, out_shape=(jax.ShapeDtypeStruct((1, ROWS, FF...  3.54 us

profile of v4, /device:TPU:1, one launch (start us, length us, event | category | flops | bytes accessed | tf_op | source)
XLA Modules:
  0.0 113.8 jit_solution(1122276283306928372)
XLA Ops:
  0.6 109.6 %shard_map.68 = (bf16[2304,256]{1,0:T(8,128)(2,1)S(1)}, f32[4608,512]{1,0:T(8,128)S(1)}, f32[2,512,256]{2,1,0:T(8,128)S(1)}, bf16[512,3072]{1,0:T(8,128)(2,1)S(1...) custom-call(s32[2,128]{1,0:T(2,128)} %bitcast.2, f32[2,128]{1,0:T(2,128)} %bitcast.3, ...), custom_call_target="tpu_custom_call" | custom-call | flops 28991029248 | bytes 15728640 | tf_op jit(solution)/shard_map/pallas_call | solution.py:396
  110.2 3.5 %shard_map.69 = (bf16[1,4608,512]{2,1,0:T(8,128)(2,1)}, bf16[1,512,3072]{2,1,0:T(8,128)(2,1)}) custom-call(bf16[2304,256]{1,0:T(8,128)(2,1)S(1)} %get-tuple-element.8.rows_in, f32[4608,512]{1,0:T(8,128)S(1)} %get-tuple-element.9.acc, f32[2,512,256]{2,1,0:T(8,128)S(1)} %get-tuple-element.10.gacc, bf16[512,3072]{1,0:T(8,128)(2,1)S(1)} %get-tuple-element.11.grad, ...), custom_call_target="tpu_custom_call" | custom-call | tf_op jit(solution)/shard_map/pallas_call | solution.py:429

commit v5 on v4

--- a/solution.py
+++ b/solution.py
@@ -236,9 +236,13 @@
         gacc[k % 2] = jnp.zeros(gacc.shape[1:], jnp.float32)
 
         def body(i, _):
-            @pl.when((c == NC - 3) & (i == 1))
+            @pl.when((c == NC - 3) & (i == 0))
             def _():
                 stage2(NC - 1, 1)
+
+            @pl.when((c == NC - 1) & (i == 1))
+            def _():
+                stage4(NC - 1, 1)
 
             multiply(k, (late + 1 + i) % 4)
             return 0
@@ -261,8 +265,6 @@
             return 0
 
         lax.fori_loop(0, 9, body, 0)
-        at = pl.ds(pl.multiple_of(part * BLK, BLK), BLK)
-        acc[at, :] = jnp.zeros((BLK, FFD), jnp.float32)
 
     load_g.wait()
     make_windows(0, 1)
@@ -270,7 +272,14 @@
     send_windows(0, 1)
     lax.fori_loop(0, 32, start_hidden, 0)
     load_w.start()
-    prep(1, 1)
+    make_windows(1, 1)
+
+    def clear(i, _):
+        acc[block_rows(i), :] = jnp.zeros((BLK, FFD), jnp.float32)
+        return 0
+
+    lax.fori_loop(0, 4, clear, 0)
+    send_windows(1, 1)
     make_windows(2, 2)
 
     def step(t, _):
@@ -281,7 +290,7 @@
             def _():
                 wide(c, fn)
 
-        stage(0, stage1)
+        stage(0, stage1, 1)
 
         @pl.when(t == 0)
         def _():
@@ -305,6 +314,10 @@
 
         stage(3, stage4, 1)
 
+        @pl.when(t == NC - 2)
+        def _():
+            stage1(NC - 1, 1)
+
         @pl.when(t == 0)
         def _():
             pltpu.make_async_copy(hb, hb, lsem.at[2]).wait()
@@ -323,7 +336,6 @@
         return 0
 
     lax.fori_loop(0, NC + 2, step, 0)
-    stage4(NC - 1, 1)
     for i in range(DONE, 4):
         if i == 3:
             for c in (NC - 2, NC - 1):

time: 114 us -> 113 us (level)
  no operation moved by 1% of the time
where the time goes in v5:
time: 113 us
  Pallas kernels  113 us (100%)
    pallas_call x1, Pallas kernels, per_device(): pl.pallas_call(gather_kernel, out_shape=(pltpu.VMEM(((4 - DONE) * BLK, 2...  109 us
    pallas_call x1, Pallas kernels, per_device(): pl.pallas_call(store_kernel, out_shape=(jax.ShapeDtypeStruct((1, ROWS, FF...  3.54 us

profile of v5, /device:TPU:1, one launch (start us, length us, event | category | flops | bytes accessed | tf_op | source)
XLA Modules:
  0.0 113.3 jit_solution(14586461668659876714)
XLA Ops:
  0.6 109.2 %shard_map.68 = (bf16[2304,256]{1,0:T(8,128)(2,1)S(1)}, f32[4608,512]{1,0:T(8,128)S(1)}, f32[2,512,256]{2,1,0:T(8,128)S(1)}, bf16[512,3072]{1,0:T(8,128)(2,1)S(1...) custom-call(s32[2,128]{1,0:T(2,128)} %bitcast.2, f32[2,128]{1,0:T(2,128)} %bitcast.3, ...), custom_call_target="tpu_custom_call" | custom-call | flops 28991029248 | bytes 15728640 | tf_op jit(solution)/shard_map/pallas_call | solution.py:408
  109.8 3.5 %shard_map.69 = (bf16[1,4608,512]{2,1,0:T(8,128)(2,1)}, bf16[1,512,3072]{2,1,0:T(8,128)(2,1)}) custom-call(bf16[2304,256]{1,0:T(8,128)(2,1)S(1)} %get-tuple-element.8.rows_in, f32[4608,512]{1,0:T(8,128)S(1)} %get-tuple-element.9.acc, f32[2,512,256]{2,1,0:T(8,128)S(1)} %get-tuple-element.10.gacc, bf16[512,3072]{1,0:T(8,128)(2,1)S(1)} %get-tuple-element.11.grad, ...), custom_call_target="tpu_custom_call" | custom-call | tf_op jit(solution)/shard_map/pallas_call | solution.py:441

commit v6 on v5

--- a/solution.py
+++ b/solution.py
@@ -308,7 +308,7 @@
             wide(t - 4, finish)
 
         stage(2, stage3)
-        @pl.when(completes(t - 4) & (t >= NC))
+        @pl.when(completes(t - 4) & (t == NC))
         def _():
             wide(t - 4, finish)
 
@@ -332,6 +332,10 @@
         @pl.when(completes(t - 2))
         def _():
             early(t - 2)
+
+        @pl.when(completes(t - 4) & (t == NC + 1))
+        def _():
+            wide(t - 4, finish)
 
         return 0
 

time: 113 us -> 113 us (level)
  no operation moved by 1% of the time
where the time goes in v6:
time: 113 us
  Pallas kernels  113 us (100%)
    pallas_call x1, Pallas kernels, per_device(): pl.pallas_call(gather_kernel, out_shape=(pltpu.VMEM(((4 - DONE) * BLK, 2...  109 us
    pallas_call x1, Pallas kernels, per_device(): pl.pallas_call(store_kernel, out_shape=(jax.ShapeDtypeStruct((1, ROWS, FF...  3.54 us

profile of v6, /device:TPU:1, one launch (start us, length us, event | category | flops | bytes accessed | tf_op | source)
XLA Modules:
  0.0 113.3 jit_solution(12516492218222855546)
XLA Ops:
  0.6 109.2 %shard_map.68 = (bf16[2304,256]{1,0:T(8,128)(2,1)S(1)}, f32[4608,512]{1,0:T(8,128)S(1)}, f32[2,512,256]{2,1,0:T(8,128)S(1)}, bf16[512,3072]{1,0:T(8,128)(2,1)S(1...) custom-call(s32[2,128]{1,0:T(2,128)} %bitcast.2, f32[2,128]{1,0:T(2,128)} %bitcast.3, ...), custom_call_target="tpu_custom_call" | custom-call | flops 28991029248 | bytes 15728640 | tf_op jit(solution)/shard_map/pallas_call | solution.py:412
  109.8 3.5 %shard_map.69 = (bf16[1,4608,512]{2,1,0:T(8,128)(2,1)}, bf16[1,512,3072]{2,1,0:T(8,128)(2,1)}) custom-call(bf16[2304,256]{1,0:T(8,128)(2,1)S(1)} %get-tuple-element.8.rows_in, f32[4608,512]{1,0:T(8,128)S(1)} %get-tuple-element.9.acc, f32[2,512,256]{2,1,0:T(8,128)S(1)} %get-tuple-element.10.gacc, bf16[512,3072]{1,0:T(8,128)(2,1)S(1)} %get-tuple-element.11.grad, ...), custom_call_target="tpu_custom_call" | custom-call | tf_op jit(solution)/shard_map/pallas_call | solution.py:445

commit v7 on v6

--- a/solution.py
+++ b/solution.py
@@ -240,10 +240,6 @@
             def _():
                 stage2(NC - 1, 1)
 
-            @pl.when((c == NC - 1) & (i == 1))
-            def _():
-                stage4(NC - 1, 1)
-
             multiply(k, (late + 1 + i) % 4)
             return 0
 
@@ -332,6 +328,10 @@
         @pl.when(completes(t - 2))
         def _():
             early(t - 2)
+
+        @pl.when(t == NC + 1)
+        def _():
+            stage4(NC - 1, 1)
 
         @pl.when(completes(t - 4) & (t == NC + 1))
         def _():

time: 113 us -> 114 us (level)
  no operation moved by 1% of the time
where the time goes in v7:
time: 114 us
  Pallas kernels  113 us (99%)
    pallas_call x1, Pallas kernels, per_device(): pl.pallas_call(gather_kernel, out_shape=(pltpu.VMEM(((4 - DONE) * BLK, 2...  109 us
    pallas_call x1, Pallas kernels, per_device(): pl.pallas_call(store_kernel, out_shape=(jax.ShapeDtypeStruct((1, ROWS, FF...  3.54 us

profile of v7, /device:TPU:1, one launch (start us, length us, event | category | flops | bytes accessed | tf_op | source)
XLA Modules:
  0.0 113.5 jit_solution(6223130226996949873)
XLA Ops:
  0.6 109.3 %shard_map.68 = (bf16[2304,256]{1,0:T(8,128)(2,1)S(1)}, f32[4608,512]{1,0:T(8,128)S(1)}, f32[2,512,256]{2,1,0:T(8,128)S(1)}, bf16[512,3072]{1,0:T(8,128)(2,1)S(1...) custom-call(s32[2,128]{1,0:T(2,128)} %bitcast.2, f32[2,128]{1,0:T(2,128)} %bitcast.3, ...), custom_call_target="tpu_custom_call" | custom-call | flops 28991029248 | bytes 15728640 | tf_op jit(solution)/shard_map/pallas_call | solution.py:412
  110.0 3.5 %shard_map.69 = (bf16[1,4608,512]{2,1,0:T(8,128)(2,1)}, bf16[1,512,3072]{2,1,0:T(8,128)(2,1)}) custom-call(bf16[2304,256]{1,0:T(8,128)(2,1)S(1)} %get-tuple-element.8.rows_in, f32[4608,512]{1,0:T(8,128)S(1)} %get-tuple-element.9.acc, f32[2,512,256]{2,1,0:T(8,128)S(1)} %get-tuple-element.10.gacc, bf16[512,3072]{1,0:T(8,128)(2,1)S(1)} %get-tuple-element.11.grad, ...), custom_call_target="tpu_custom_call" | custom-call | tf_op jit(solution)/shard_map/pallas_call | solution.py:445
